TPU v7x, 32 devices: a whole 2x2x4 slice. The times are simulated.
32 devices in a mesh: group: 2 (over x), seq: 16 (over z, y, core).
Axes of the slice: x: 2, y: 2, z: 4, core: 2. Of those that a mesh axis runs over, the one named last changes fastest.
Arguments:
- queries: bfloat16 [96, 128, 2560], P(('group', 'seq')), parts along dimension 0, may hold values from -9 to 9
- keys: bfloat16 [96, 128, 2560], P(('group', 'seq')), parts along dimension 0, may hold values from -9 to 9
- values: bfloat16 [96, 128, 2560], P(('group', 'seq')), parts along dimension 0, may hold values from -6 to 6
- block_list: int32 [96, 20, 2], P('group'), parts along dimension 0, may hold values from 0 to 47, as said below
- list_len: int32 [96, 20], P('group'), parts along dimension 0, may hold values from 0 to 2, as said below
- window_time: int32 [20], replicated, may hold values from 0 to 1
- window_rows: int32 [20], replicated, may hold values from 0 to 1
Outputs:
- attention_out: bfloat16 [96, 128, 2560], P(('group', 'seq')), parts along dimension 0
There are 2 independent parts, one for each index of `group`. A program takes and returns all parts, laid end to end along the dimension named above; an argument that names none is the same for every part. Nothing has to cross between parts.
Inputs may be any that keep to these rules, and one draw needn't show every extreme that they name: `block_list`: for the 3 query tiles of one block and one head, all listed tiles lie on a single other block, and together the used entries name exactly 2 distinct tiles; one list's entries are distinct. For the query tiles of one block, no other block holds listed tiles of more than 2 heads, and some block holds those of exactly 2 heads, so the distinct listed pairs of tile and head of one block on another block number at most 4, reached in every draw. Entries of block_list at and after position list_len are not used.
All inputs are finite; a program needn't handle non-finite values.
Results may differ from a plain program's by a relative error of at most 0.0032.
Values may be sent and summed in bfloat16 or wider, within the bound.
A program may use at most 128 MiB of HBM per device.

v0:
```python
import math

import jax
import jax.numpy as jnp
from jax import lax
from jax.sharding import PartitionSpec as P

TIME_TILES = 1
ROW_TILES = 3
ROW_BLOCKS = 2
LIST = 2


BIG_NEG = -1e30


def from_partner(block, axis, apart):
    count = lax.axis_size(axis)
    route = []
    for low in range(count):
        high = low | 1 << apart
        if high != low and high < count:
            route += [(low, high), (high, low)]
    return lax.ppermute(block, axis, route)


def passed_along(value, axis, steps):
    count = lax.axis_size(axis)
    initial, last = (max(0, -steps), min(count, count - steps))
    return lax.ppermute(value, axis, [(source, source + steps) for source in range(initial, last)])


def halo_paired(key_block, val_block, row_pos):
    edge_key = jnp.where(row_pos == 0, key_block[:, ROW_TILES - 1], key_block[:, 0])
    edge_val = jnp.where(row_pos == 0, val_block[:, ROW_TILES - 1], val_block[:, 0])
    got_key, got_val = from_partner((edge_key, edge_val), "seq", 0)
    middle_shape = (TIME_TILES, ROW_TILES + 2) + key_block.shape[2:]
    middle_key = jnp.zeros(middle_shape, key_block.dtype).at[:, 1 : ROW_TILES + 1].set(key_block)
    middle_val = jnp.zeros(middle_shape, val_block.dtype).at[:, 1 : ROW_TILES + 1].set(val_block)
    blank_key = jnp.zeros_like(got_key)
    blank_val = jnp.zeros_like(got_val)
    middle_key = middle_key.at[:, 0].set(jnp.where(row_pos == 1, got_key, blank_key))
    middle_val = middle_val.at[:, 0].set(jnp.where(row_pos == 1, got_val, blank_val))
    middle_key = middle_key.at[:, ROW_TILES + 1].set(jnp.where(row_pos == 0, got_key, blank_key))
    middle_val = middle_val.at[:, ROW_TILES + 1].set(jnp.where(row_pos == 0, got_val, blank_val))
    start = jnp.where(row_pos == 0, 1, 0).astype(jnp.int32)
    shape = (TIME_TILES + 2, ROW_TILES + 2) + key_block.shape[2:]
    key_ext = jnp.zeros(shape, key_block.dtype).at[1 : TIME_TILES + 1].set(middle_key)
    val_ext = jnp.zeros(shape, val_block.dtype).at[1 : TIME_TILES + 1].set(middle_val)
    zero_index = jnp.int32(0)
    for distance, source, target in (
        (ROW_BLOCKS, TIME_TILES - 1, 0),
        (-ROW_BLOCKS, 0, TIME_TILES + 1),
    ):
        band_key = lax.dynamic_slice_in_dim(middle_key, start, ROW_TILES + 1, 1)
        band_val = lax.dynamic_slice_in_dim(middle_val, start, ROW_TILES + 1, 1)
        recv_key, recv_val = passed_along((band_key, band_val), "seq", distance)
        where_to = (jnp.int32(target), start, zero_index, zero_index)
        key_ext = lax.dynamic_update_slice(key_ext, recv_key, where_to)
        val_ext = lax.dynamic_update_slice(val_ext, recv_val, where_to)
    return (key_ext, val_ext)


def on_device(queries, keys, values, block_list, list_len, window_time, window_rows):
    tiles_dev, tile_len, feat = queries.shape
    heads = window_time.shape[0]
    head_dim = feat // heads
    tiles_total = block_list.shape[0]
    blocks = lax.axis_size("seq")
    device = lax.axis_index("seq")
    time_block = device // ROW_BLOCKS
    row_pos = device % ROW_BLOCKS
    key_block = keys.reshape((TIME_TILES, ROW_TILES) + keys.shape[1:])
    val_block = values.reshape((TIME_TILES, ROW_TILES) + values.shape[1:])
    key_ext, val_ext = halo_paired(key_block, val_block, row_pos)
    time_count = TIME_TILES * blocks // ROW_BLOCKS
    row_count = ROW_BLOCKS * ROW_TILES
    ext_cols = ROW_TILES + 2
    ext_time = time_block * TIME_TILES + jnp.arange(TIME_TILES + 2, dtype=jnp.int32) - 1
    ext_row = row_pos * ROW_TILES + jnp.arange(ext_cols, dtype=jnp.int32) - 1
    ext_valid = ((ext_time >= 0) & (ext_time < time_count))[:, None] & (
        (ext_row >= 0) & (ext_row < row_count)
    )[None, :]
    valid_rows = jnp.stack([ext_valid[a : a + TIME_TILES] for a in range(3)], axis=1)
    col_gap = jnp.abs(
        jnp.arange(ext_cols, dtype=jnp.int32)[None, :]
        - jnp.arange(ROW_TILES, dtype=jnp.int32)[:, None]
        - 1
    )
    time_gap = jnp.abs(jnp.arange(3, dtype=jnp.int32) - 1)
    far_min = blocks - 1
    per_source = (heads + far_min - 1) // far_min
    capacity = per_source * LIST
    pair_count = heads * tiles_dev
    all_live = jnp.arange(LIST, dtype=jnp.int32)[None, None, :] < list_len[:, :, None]
    local_ids = block_list - device * tiles_dev
    mine = all_live & (local_ids >= 0) & (local_ids < tiles_dev)
    wanted = (local_ids[..., None] == jnp.arange(tiles_dev, dtype=jnp.int32)) & mine[..., None]
    wanted = jnp.any(wanted, axis=2).reshape(blocks, tiles_dev, heads, tiles_dev)
    request = jnp.any(wanted, axis=1).reshape(blocks, pair_count).astype(jnp.int32)
    order_num = jnp.cumsum(request, axis=1) - request
    chosen = (order_num[:, None, :] == jnp.arange(capacity, dtype=jnp.int32)[None, :, None]) & (
        request[:, None, :] > 0
    )
    flat_pick = jnp.sum(
        chosen.astype(jnp.int32) * jnp.arange(pair_count, dtype=jnp.int32)[None, None, :], axis=2
    )
    pick_head = flat_pick // tiles_dev
    pick_tile = flat_pick % tiles_dev
    split_keys = keys.reshape(tiles_dev, tile_len, heads, head_dim)
    split_vals = values.reshape(tiles_dev, tile_len, heads, head_dim)
    send_key = split_keys[pick_tile, :, pick_head, :]
    send_val = split_vals[pick_tile, :, pick_head, :]
    recv_key, recv_val = (
        lax.all_to_all(send_key, "seq", split_axis=0, concat_axis=0, tiled=True),
        lax.all_to_all(send_val, "seq", split_axis=0, concat_axis=0, tiled=True),
    )
    own_list = lax.dynamic_slice_in_dim(block_list, device * tiles_dev, tiles_dev, 0)
    own_len = lax.dynamic_slice_in_dim(list_len, device * tiles_dev, tiles_dev, 0)
    own_live = jnp.arange(LIST, dtype=jnp.int32)[None, None, :] < own_len[:, :, None]
    hits = (own_list[..., None] == jnp.arange(tiles_total, dtype=jnp.int32)) & own_live[..., None]
    asked = jnp.any(hits, axis=(0, 2)).reshape(heads, blocks, tiles_dev)
    asked = jnp.transpose(asked, (1, 0, 2)).reshape(blocks, pair_count).astype(jnp.int32)
    slot_table = jnp.cumsum(asked, axis=1) - asked
    source_ids = own_list // tiles_dev
    column_ids = (
        jnp.arange(heads, dtype=jnp.int32)[None, :, None] * tiles_dev + own_list % tiles_dev
    )
    slot_ids = slot_table[source_ids, column_ids]
    scale = 1.0 / math.sqrt(head_dim)

    def head_major(extended):
        moved = extended.reshape(TIME_TILES + 2, ext_cols * tile_len, heads, head_dim)
        return jnp.transpose(moved, (2, 0, 1, 3))

    key_heads = head_major(key_ext)
    val_heads = head_major(val_ext)
    key_windows = jnp.concatenate([key_heads[:, a : a + TIME_TILES] for a in range(3)], axis=2)
    val_windows = jnp.concatenate([val_heads[:, a : a + TIME_TILES] for a in range(3)], axis=2)
    query_heads = jnp.transpose(
        queries.reshape(TIME_TILES, ROW_TILES * tile_len, heads, head_dim), (2, 0, 1, 3)
    )
    far_keys = recv_key[source_ids, slot_ids]
    far_vals = recv_val[source_ids, slot_ids]
    far_key_heads = jnp.transpose(far_keys, (1, 0, 2, 3, 4)).reshape(
        heads, tiles_dev, LIST * tile_len, head_dim
    )
    far_val_heads = jnp.transpose(far_vals, (1, 0, 2, 3, 4)).reshape(
        heads, tiles_dev, LIST * tile_len, head_dim
    )
    far_live = jnp.transpose(own_live, (1, 0, 2))
    span_tiles = 3 * ext_cols

    def one_head(inputs):
        query_one, key_win, val_win, far_key, far_val, reach_time, reach_rows, live_one = inputs
        win_ok = (
            valid_rows[:, None, :, :]
            & (col_gap[None, :, None, :] <= jnp.minimum(reach_rows, 1))
            & (time_gap[None, None, :, None] <= reach_time)
        )
        win_ok = win_ok.reshape(tiles_dev, 1, span_tiles, 1)
        near = (
            jnp.einsum("tqd,tkd->tqk", query_one, key_win, preferred_element_type=jnp.float32)
            * scale
        )
        near = near.reshape(tiles_dev, tile_len, span_tiles, tile_len)
        near = jnp.where(win_ok, near, BIG_NEG).reshape(tiles_dev, tile_len, span_tiles * tile_len)
        query_tiles = query_one.reshape(tiles_dev, tile_len, head_dim)
        far = (
            jnp.einsum("txd,tyd->txy", query_tiles, far_key, preferred_element_type=jnp.float32)
            * scale
        )
        far_ok = jnp.repeat(live_one, tile_len, axis=1)[:, None, :]
        far = jnp.where(far_ok, far, BIG_NEG)
        top = jnp.maximum(jnp.max(near, axis=2, keepdims=True), jnp.max(far, axis=2, keepdims=True))
        near_weights = jnp.exp(near - top)
        far_weights = jnp.exp(far - top)
        total = jnp.sum(near_weights, axis=2, keepdims=True) + jnp.sum(
            far_weights, axis=2, keepdims=True
        )
        near_rounded = near_weights.astype(jnp.bfloat16).reshape(
            TIME_TILES, ROW_TILES * tile_len, span_tiles * tile_len
        )
        mixed = jnp.einsum(
            "tqk,tkd->tqd", near_rounded, val_win, preferred_element_type=jnp.float32
        )
        mixed = mixed.reshape(tiles_dev, tile_len, head_dim)
        mixed = mixed + jnp.einsum(
            "txy,tyd->txd",
            far_weights.astype(jnp.bfloat16),
            far_val,
            preferred_element_type=jnp.float32,
        )
        return (mixed / total).astype(jnp.bfloat16)

    results = lax.map(
        one_head,
        (
            query_heads,
            key_windows,
            val_windows,
            far_key_heads,
            far_val_heads,
            window_time,
            window_rows,
            far_live,
        ),
    )
    return jnp.transpose(results, (1, 2, 0, 3)).reshape(tiles_dev, tile_len, feat)


def solution(mesh):
    return jax.shard_map(
        on_device,
        mesh=mesh,
        in_specs=(
            P(("group", "seq"), None, None),
            P(("group", "seq"), None, None),
            P(("group", "seq"), None, None),
            P("group", None, None),
            P("group", None),
            P(),
            P(),
        ),
        out_specs=P(("group", "seq"), None, None),
        check_vma=False,
    )
```

profile of v0, /device:TPU:13, one launch (start us, length us, event | category | flops | bytes accessed | tf_op | source)
XLA Modules:
  0.0 666.2 jit_solution(11511797322227470170)
XLA Ops:
  0.0 2.4 fusion.30
  3.1 2.2 fusion.31
  5.8 2.3 copy.85
  8.8 2.8 copy.95
  11.6 2.1 gather_fusion
  13.7 6.4 all-to-all-start
  20.3 1.8 scatter.34
  24.1 1.7 constant_dynamic-slice_fusion.3
  25.8 3.1 collective-permute-start.4
  29.8 1.7 gather_fusion.1
  31.8 2.2 collective-permute-start.5
  34.0 3.5 scatter.26
  37.5 3.9 copy.109
  41.6 4.0 copy.110
  45.6 3.7 gather_fusion.3
  49.4 4.4 reshape.609
  53.8 3.5 copy.111
  58.7 1.6 constant_dynamic-slice_fusion.6
  60.3 4.0 collective-permute-start.1
  64.5 4.5 scatter.39
  69.0 4.6 scatter.31
  73.6 1.9 collective-permute-start.2
  75.6 136.9 %collective-permute-done.4 = bf16[1,4,128,2560]{3,2,1,0:T(8,128)(2,1)} collective-permute-done((bf16[1,4,128,2560]{3,2,1,0:T(8,128)(2,1)}, bf16[1,4,128,2560]{3,2,1,0:T(8,128)(2,1)}, u32[]{:S(2)}, u32[]{:S(2)}) %collective-permute-start.4) | collective-permute-done | bytes 2621472 | tf_op jit(solution)/shard_map/ppermute | solution.py:30
  212.5 3.5 constant_dynamic-update-slice_fusion.2
  216.0 6.1 all-to-all-start.1
  222.1 3.4 constant_dynamic-update-slice_fusion.1
  225.5 17.1 %reshape.620 = bf16[3,640,20,128]{3,2,1,0:T(8,128)(2,1)} reshape(bf16[3,5,128,2560]{3,2,1,0:T(8,128)(2,1)} %constant_dynamic-update-slice_fusion.1) | data formatting | bytes 19660800 | tf_op jit(solution)/shard_map/reshape | solution.py:133
  242.6 5.5 fusion.55
  248.1 60.3 %pad_maximum_fusion.1 = bf16[20,1,1920,128]{3,0,2,1:T(8,128)(2,1)} fusion(bf16[20,1,640,128]{3,0,2,1:T(8,128)(2,1)S(1)} %get-tuple-element.260, bf16[20,1,640,128]{3,0,2,1:T(8,128)(2,1)S(1)} %get-tuple-element.261, bf16[20,1,640,128]{3,0,2,1:T(8,128)(2,1)S(1)} %get-tuple-element.259), kind=kLoop, calls=%fused_computation.50 | loop fusion | flops 9830400 | bytes 19660800 | tf_op jit(solution)/shard_map/concatenate | solution.py:139
  308.4 10.1 %copy.114 = bf16[20,1,1920,128]{3,2,1,0:T(8,128)(2,1)} copy(bf16[20,1,1920,128]{3,0,2,1:T(8,128)(2,1)} %pad_maximum_fusion.1) | data formatting | bytes 19660800
  318.5 3.4 constant_dynamic-update-slice_fusion.4
  321.9 3.5 constant_dynamic-update-slice_fusion.3
  325.4 17.1 %reshape.613 = bf16[3,640,20,128]{3,2,1,0:T(8,128)(2,1)} reshape(bf16[3,5,128,2560]{3,2,1,0:T(8,128)(2,1)} %constant_dynamic-update-slice_fusion.3) | data formatting | bytes 19660800 | tf_op jit(solution)/shard_map/reshape | solution.py:133
  342.6 5.5 fusion.56
  348.1 60.3 %pad_maximum_fusion = bf16[20,1,1920,128]{3,0,2,1:T(8,128)(2,1)} fusion(bf16[20,1,640,128]{3,0,2,1:T(8,128)(2,1)S(1)} %get-tuple-element.263, bf16[20,1,640,128]{3,0,2,1:T(8,128)(2,1)S(1)} %get-tuple-element.264, bf16[20,1,640,128]{3,0,2,1:T(8,128)(2,1)S(1)} %get-tuple-element.262), kind=kLoop, calls=%fused_computation.49 | loop fusion | flops 9830400 | bytes 19660800 | tf_op jit(solution)/shard_map/concatenate | solution.py:138
  408.4 10.2 %copy.112 = bf16[20,1,1920,128]{3,2,1,0:T(8,128)(2,1)} copy(bf16[20,1,1920,128]{3,0,2,1:T(8,128)(2,1)} %pad_maximum_fusion) | data formatting | bytes 19660800
  418.6 4.9 gather_fusion.2
  423.5 3.3 gather_fusion.4
  426.8 235.0 %while.20 = (s32[]{:T(128)}, bf16[20,3,128,128]{2,3,0,1:T(8,128)(2,1)}, pred[1,3,5]{2,1,0:T(4,128)(4,1)}, s32[20]{0:T(128)S(1)}, s32[20]{0:T(128)S(1)}, /*index=...) while((s32[]{:T(128)}, ...), condition=%wide.wide.region_11.12_spmd.clone, body=%wide.wide.region_6.11_spmd.clone.sunk | while | flops 433078048 | bytes 14210132 | solution.py:196
  429.9 1.8 fusion.89
  441.7 1.8 fusion.89
  446.7 1.6 fusion.93
  453.4 1.8 fusion.89
  465.2 1.8 fusion.89
  476.9 1.8 fusion.89
  481.9 1.6 fusion.93
  488.7 1.8 fusion.89
  500.4 1.8 fusion.89
  512.2 1.8 fusion.89
  523.9 1.8 fusion.89
  535.7 1.8 fusion.89
  540.7 1.6 fusion.93
  547.4 1.8 fusion.89
  559.2 1.8 fusion.89
  570.9 1.8 fusion.89
  576.0 1.6 fusion.93
  582.7 1.8 fusion.89
  594.4 1.8 fusion.89
  606.2 1.8 fusion.89
  617.9 1.8 fusion.89
  629.7 1.8 fusion.89
  641.4 1.8 fusion.89
  653.2 1.8 fusion.89
  661.8 4.0 copy.117
  (597 shorter events, 184.8 us)
Async XLA Ops:
  0.0 5.8 copy-start.1
  0.0 5.3 copy-start.3
  0.0 5.3 copy-start.2
  2.4 20.4 %collective-permute-start.3 = (bf16[1,128,2560]{2,1,0:T(8,128)(2,1)}, bf16[1,128,2560]{2,1,0:T(8,128)(2,1)}, u32[]{:S(2)}, u32[]{:S(2)}) collective-permute-start(bf16[1,128,2560]{2,1,0:T(8,128)(2,1)} %fusion.30), channel_id=1, source_target_pairs={{0,1},{1,0},{2,3},{3,2},{4,5},{5,4},{6,7},{7,6},{8,9},{9,8},{10,11... | collective-permute-start | bytes 1966088 | tf_op jit(solution)/shard_map/ppermute | solution.py:24
  5.3 52.1 %collective-permute-start = (bf16[1,128,2560]{2,1,0:T(8,128)(2,1)}, bf16[1,128,2560]{2,1,0:T(8,128)(2,1)}, u32[]{:S(2)}, u32[]{:S(2)}) collective-permute-start(bf16[1,128,2560]{2,1,0:T(8,128)(2,1)} %fusion.31), channel_id=1, source_target_pairs={{0,1},{1,0},{2,3},{3,2},{4,5},{5,4},{6,7},{7,6},{8,9},{9,8},{10,11... | collective-permute-start | bytes 1966088 | tf_op jit(solution)/shard_map/ppermute | solution.py:24
  13.7 202.3 %all-to-all-start = ((bf16[16,4,128,128]{3,2,1,0:T(8,128)(2,1)}), bf16[16,4,128,128]{3,2,1,0:T(8,128)(2,1)}, u32[]{:S(2)}, u32[]{:S(2)}) async-start(bf16[16,4,128,128]{3,2,1,0:T(8,128)(2,1)} %bitcast.205), calls=%async_computation | async-start | bytes 4194304 | tf_op jit(solution)/shard_map/all_to_all | solution.py:115
  25.8 186.7 %collective-permute-start.4 = (bf16[1,4,128,2560]{3,2,1,0:T(8,128)(2,1)}, bf16[1,4,128,2560]{3,2,1,0:T(8,128)(2,1)}, u32[]{:S(2)}, u32[]{:S(2)}) collective-permute-start(bf16[1,4,128,2560]{3,2,1,0:T(8,128)(2,1)} %constant_dynamic-slice_fusion.3), channel_id=1, source_target_pairs={{0,2},{1,3},{2,4},{3,5},{4,6},{5,7},{6,8},{7,9},{8,10},{9,11},{10,... | collective-permute-start | bytes 7864328 | tf_op jit(solution)/shard_map/ppermute | solution.py:30
  31.8 190.4 %collective-permute-start.5 = (bf16[1,4,128,2560]{3,2,1,0:T(8,128)(2,1)}, bf16[1,4,128,2560]{3,2,1,0:T(8,128)(2,1)}, u32[]{:S(2)}, u32[]{:S(2)}) collective-permute-start(bf16[1,4,128,2560]{3,2,1,0:T(8,128)(2,1)} %constant_dynamic-slice_fusion.3), channel_id=1, source_target_pairs={{2,0},{3,1},{4,2},{5,3},{6,4},{7,5},{8,6},{9,7},{10,8},{11,9},{12,... | collective-permute-start | bytes 7864328 | tf_op jit(solution)/shard_map/ppermute | solution.py:30
  34.0 15.4 %copy-start.4 = (pred[1,3,5]{2,1,0:T(4,128)(4,1)}, pred[1,3,5]{2,1,0:T(4,128)(4,1)S(1)}, u32[]{:S(2)}) copy-start(pred[1,3,5]{2,1,0:T(4,128)(4,1)S(1)} %pad_add_fusion) | copy-start | bytes 49
  53.8 3.5 copy-start
  60.3 258.2 %collective-permute-start.1 = (bf16[1,4,128,2560]{3,2,1,0:T(8,128)(2,1)}, bf16[1,4,128,2560]{3,2,1,0:T(8,128)(2,1)}, u32[]{:S(2)}, u32[]{:S(2)}) collective-permute-start(bf16[1,4,128,2560]{3,2,1,0:T(8,128)(2,1)} %constant_dynamic-slice_fusion.6), channel_id=1, source_target_pairs={{0,2},{1,3},{2,4},{3,5},{4,6},{5,7},{6,8},{7,9},{8,10},{9,11},{10,... | collective-permute-start | bytes 7864328 | tf_op jit(solution)/shard_map/ppermute | solution.py:30
  73.6 248.3 %collective-permute-start.2 = (bf16[1,4,128,2560]{3,2,1,0:T(8,128)(2,1)}, bf16[1,4,128,2560]{3,2,1,0:T(8,128)(2,1)}, u32[]{:S(2)}, u32[]{:S(2)}) collective-permute-start(bf16[1,4,128,2560]{3,2,1,0:T(8,128)(2,1)} %constant_dynamic-slice_fusion.6), channel_id=1, source_target_pairs={{2,0},{3,1},{4,2},{5,3},{6,4},{7,5},{8,6},{9,7},{10,8},{11,9},{12,... | collective-permute-start | bytes 7864328 | tf_op jit(solution)/shard_map/ppermute | solution.py:30
  216.0 207.5 %all-to-all-start.1 = ((bf16[16,4,128,128]{3,2,1,0:T(8,128)(2,1)}), bf16[16,4,128,128]{3,2,1,0:T(8,128)(2,1)S(1)}, u32[]{:S(2)}, u32[]{:S(2)}) async-start(bf16[16,4,128,128]{3,2,1,0:T(8,128)(2,1)} %bitcast.206), calls=%async_computation.1 | async-start | bytes 4194304 | tf_op jit(solution)/shard_map/all_to_all | solution.py:116
  423.5 3.3 copy-start.5
  423.5 3.3 copy-start.6
where the time goes:
time: 678 us; the launch traced here: 666 us
  local copies, waits for them, and re-layouts  214 us (32%)
  other arithmetic  159 us (23%)
  waiting for transfers between devices  137 us (20%)
  matrix products  118 us (17%)
  starting transfers between devices  24.3 us (4%)
  loops' own time  14 us (2%)
    ppermute x4, waiting for transfers between devices, passed_along(): lax.ppermute(value, axis, [(source, source + steps) for source in range(i...  137 us
    concatenate x1, other arithmetic, on_device(): jnp.concatenate([key_heads[:, a:a + TIME_TILES] for a in range(3)], axis=2)  60.3 us
    concatenate x1, other arithmetic, on_device(): jnp.concatenate([val_heads[:, a:a + TIME_TILES] for a in range(3)], axis=2)  60.3 us
    dynamic_slice x60, local copies, waits for them, and re-layouts, on_device(): lax.map(one_head, (query_heads, key_windows, val_windows, far_key_heads,...  43.6 us
    dot_general x20, matrix products, one_head(): jnp.einsum('tqd,tkd->tqk', query_one, key_win, preferred_element_type=jnp...  36.9 us
    reshape x2, local copies, waits for them, and re-layouts, head_major(): extended.reshape(TIME_TILES + 2, ext_cols * tile_len, heads, head_dim)  34.3 us
    dot_general x20, matrix products, one_head(): jnp.einsum('tqk,tkd->tqd', near_rounded, val_win, preferred_element_type=...  31.7 us
    unnamed x19, local copies, waits for them, and re-layouts  30 us
  transfers between devices with their start and end apart: 8, of which 1 were waited for; matrix products, arithmetic and copies ran while one was open for 39% of the time, Pallas kernels for 0%

commit v1 on v0

v1 whole, which is shorter than its diff:
```python
import functools
import math

import jax
import jax.numpy as jnp
from jax import lax
from jax.experimental import pallas as pl
from jax.experimental.pallas import tpu as pltpu
from jax.sharding import PartitionSpec as P

ROW_TILES = 3
ROW_BLOCKS = 2
LIST = 2
CHUNK_HEADS = 4
BIG_NEG = -1e30


def kernel(
    blocks, heads, tok, dim, per_source,
    send_meta, recv_meta, biases, q_hbm, k_hbm, v_hbm, out_ref,
    qs, kv, edge, near, near_edge, relayed, relayed_edge, far_out, far_in, acc, top, total,
    load_sem, edge_sem, near_sem, near_edge_sem, relay_sem, relay_edge_sem, far_sem,
):
    me = lax.axis_index("seq")
    side = lax.rem(me, ROW_BLOCKS)
    time = me // ROW_BLOCKS
    times = blocks // ROW_BLOCKS
    odd = lax.rem(time, 2)
    partner = me + 1 - 2 * side
    mirror = me + ROW_BLOCKS * (1 - 2 * odd)
    ahead = 2 * (1 - 2 * odd)
    gives = jnp.logical_and(time + ahead >= 0, time + ahead < times)
    takes = jnp.logical_and(time - ahead >= 0, time - ahead < times)
    relay_to = me + ROW_BLOCKS * ahead
    edge_tile = 2 - 2 * side
    other_tile = 2 * side
    chunks = heads // CHUNK_HEADS

    def remote(src, dst, sems, device):
        return pltpu.make_async_remote_copy(
            src_ref=src, dst_ref=dst, send_sem=sems.at[0], recv_sem=sems.at[1],
            device_id={"seq": device}, device_id_type=pl.DeviceIdType.MESH,
        )

    def part_of(chunk):
        return pl.ds(chunk * CHUNK_HEADS, CHUNK_HEADS)

    def near_copy(chunk):
        part = part_of(chunk)
        return remote(kv.at[:, part], near.at[:, part], near_sem.at[chunk], mirror)

    def near_edge_copy(chunk):
        part = part_of(chunk)
        return remote(
            near.at[:, part, edge_tile], near_edge.at[:, part],
            near_edge_sem.at[chunk], partner,
        )

    def relay_copy(chunk):
        part = part_of(chunk)
        return remote(
            near.at[:, part], relayed.at[:, part], relay_sem.at[chunk], relay_to
        )

    def relay_edge_copy(chunk):
        part = part_of(chunk)
        return remote(
            relayed.at[:, part, edge_tile], relayed_edge.at[:, part],
            relay_edge_sem.at[chunk], partner,
        )

    def far_copy(offset):
        return remote(
            far_out.at[offset], far_in.at[offset], far_sem.at[offset], lax.rem(me + offset, blocks)
        )

    def loads(head):
        cols = pl.ds(pl.multiple_of(head * dim, dim), dim)
        return [
            pltpu.make_async_copy(array.at[:, :, cols], held, load_sem.at[which, head])
            for which, (array, held) in enumerate(
                ((k_hbm, kv.at[0, head]), (v_hbm, kv.at[1, head]), (q_hbm, qs.at[head]))
            )
        ]

    def start_loads(head, carry):
        for copy in loads(head):
            copy.start()
        return carry

    def end_loads(head, carry):
        for copy in loads(head):
            copy.wait()
        return carry

    lax.fori_loop(0, heads, start_loads, 0)
    barrier = pltpu.get_barrier_semaphore()

    def greet(offset, carry):
        pl.semaphore_signal(
            barrier, inc=1, device_id={"seq": lax.rem(me + offset, blocks)},
            device_id_type=pl.DeviceIdType.MESH,
        )
        return carry

    lax.fori_loop(1, blocks, greet, 0)
    lax.fori_loop(0, heads, end_loads, 0)
    pl.semaphore_wait(barrier, blocks - 1)

    edge_copy = remote(kv.at[:, :, edge_tile], edge, edge_sem, partner)
    edge_copy.start()

    def start_near(chunk, carry):
        near_copy(chunk).start()
        return carry

    lax.fori_loop(0, chunks, start_near, 0)

    def start_far(offset, carry):
        target = lax.rem(me + offset, blocks)
        for pair in range(per_source):
            head = send_meta[target, 3 * pair]
            for which in range(LIST):
                tile = send_meta[target, 3 * pair + 1 + which]
                for part in range(2):
                    far_out[offset, pair * LIST + which, part] = kv[part, head, tile]
        far_copy(offset).start()
        return carry

    lax.fori_loop(1, blocks, start_far, 0)

    factor = math.log2(math.e) / math.sqrt(dim)

    def scores_of(query, key, bias):
        product = lax.dot_general(
            query, key, (((1,), (1,)), ((), ())), preferred_element_type=jnp.float32
        )
        return product * factor + bias

    def fold(head, tile, scores, value, first):
        high = jnp.max(scores, axis=1, keepdims=True)
        if not first:
            old = top[head, tile]
            high = jnp.maximum(high, old)
            shrink = jnp.exp2(old - high)
        weights = jnp.exp2(scores - high)
        amount = jnp.sum(weights, axis=1, keepdims=True)
        mixed = jnp.dot(
            weights.astype(jnp.bfloat16), value, preferred_element_type=jnp.float32
        )
        if not first:
            amount = amount + total[head, tile] * shrink
            mixed = mixed + acc[head, tile] * shrink
        return high, amount, mixed

    def keep(head, tile, state):
        top[head, tile], total[head, tile], acc[head, tile] = state

    def window_row(head, rows, edges, own):
        along = jnp.float32(0.0) if own else biases[0, head]
        lane = lax.broadcasted_iota(jnp.int32, (1, 3 * tok), 1)
        bias = jnp.where(lane < tok, along, biases[1 if own else 2, head])
        k_mid, v_mid = rows[0, head, 1], rows[1, head, 1]
        k_edge, v_edge = rows[0, head, edge_tile], rows[1, head, edge_tile]
        k_other, v_other = rows[0, head, other_tile], rows[1, head, other_tile]
        k_out, v_out = edges[0, head], edges[1, head]
        for tile, key, value in (
            (1, (k_mid, k_edge, k_other), (v_mid, v_edge, v_other)),
            (edge_tile, (k_edge, k_mid, k_out), (v_edge, v_mid, v_out)),
            (other_tile, (k_other, k_mid), (v_other, v_mid)),
        ):
            key = jnp.concatenate(key, axis=0)
            value = jnp.concatenate(value, axis=0)
            scores = scores_of(qs[head, tile], key, bias[:, : key.shape[0]])
            keep(head, tile, fold(head, tile, scores, value, own))

    edge_copy.wait_recv()

    def own_row(head, carry):
        window_row(head, kv, edge, True)
        return carry

    lax.fori_loop(0, heads, own_row, 0)

    def near_rows(chunk):
        def step(inner, carry):
            window_row(chunk * CHUNK_HEADS + inner, near, near_edge, False)
            return carry

        lax.fori_loop(0, CHUNK_HEADS, step, 0)

    def relayed_rows(chunk):
        def step(inner, carry):
            window_row(chunk * CHUNK_HEADS + inner, relayed, relayed_edge, False)
            return carry

        lax.fori_loop(0, CHUNK_HEADS, step, 0)

    def relay_arrived(chunk):
        relay_copy(chunk).wait_recv()
        relay_edge_copy(chunk).start()

    def relay_used(chunk):
        relay_edge_copy(chunk).wait_recv()
        relayed_rows(chunk)

    def time_chunk(chunk, carry):
        near_copy(chunk).wait_recv()
        near_edge_copy(chunk).start()

        @pl.when(gives)
        def _():
            relay_copy(chunk).start()

        @pl.when(jnp.logical_and(takes, chunk > 0))
        def _():
            relay_arrived(chunk - 1)

        near_edge_copy(chunk).wait_recv()
        near_rows(chunk)

        @pl.when(jnp.logical_and(takes, chunk > 0))
        def _():
            relay_used(chunk - 1)

        return carry

    lax.fori_loop(0, chunks, time_chunk, 0)

    @pl.when(takes)
    def _():
        relay_arrived(chunks - 1)
        relay_used(chunks - 1)

    def far_arrived(offset, carry):
        far_copy(offset).wait_recv()
        return carry

    lax.fori_loop(1, blocks, far_arrived, 0)

    def far_head(head, carry):
        cols = pl.ds(pl.multiple_of(head * dim, dim), dim)
        offset, slot = recv_meta[0, head], recv_meta[1, head]
        key = jnp.concatenate([far_in[offset, slot + w, 0] for w in range(LIST)], axis=0)
        value = jnp.concatenate([far_in[offset, slot + w, 1] for w in range(LIST)], axis=0)
        lane = lax.broadcasted_iota(jnp.int32, (1, LIST * tok), 1)
        for tile in range(ROW_TILES):
            bias = jnp.where(lane < tok, biases[3 + 2 * tile, head], biases[4 + 2 * tile, head])
            scores = scores_of(qs[head, tile], key, bias)
            _, amount, mixed = fold(head, tile, scores, value, False)
            out_ref[tile, :, cols] = (mixed / amount).astype(out_ref.dtype)
        return carry

    lax.fori_loop(0, heads, far_head, 0)

    edge_copy.wait_send()

    def sent(chunk, carry):
        near_copy(chunk).wait_send()
        near_edge_copy(chunk).wait_send()

        @pl.when(gives)
        def _():
            relay_copy(chunk).wait_send()

        @pl.when(takes)
        def _():
            relay_edge_copy(chunk).wait_send()

        return carry

    lax.fori_loop(0, chunks, sent, 0)

    def far_sent(offset, carry):
        far_copy(offset).wait_send()
        return carry

    lax.fori_loop(1, blocks, far_sent, 0)


def listed(block_list, list_len, window_time, window_rows, blocks, heads, per_source):
    me = lax.axis_index("seq")
    lists = block_list.reshape(blocks, ROW_TILES, heads, LIST)
    lens = list_len.reshape(blocks, ROW_TILES, heads, 1)
    live = jnp.arange(LIST, dtype=jnp.int32) < lens
    low = jnp.min(jnp.where(live, lists, jnp.int32(1 << 20)), axis=(1, 3))
    high = jnp.max(jnp.where(live, lists, jnp.int32(-1)), axis=(1, 3))
    source = low // ROW_TILES
    low_tile, high_tile = low % ROW_TILES, high % ROW_TILES
    number = jnp.arange(heads, dtype=jnp.int32)[None, :]
    mine = source == me
    first = jnp.min(jnp.where(mine, number, heads), axis=1, keepdims=True)
    first = jnp.where(first == heads, 0, first)
    last = jnp.max(jnp.where(mine, number, 0), axis=1, keepdims=True)
    columns = []
    for pick in (first, last)[:per_source]:
        hit = number == pick
        columns += [
            pick[:, 0],
            jnp.sum(jnp.where(hit, low_tile, 0), axis=1),
            jnp.sum(jnp.where(hit, high_tile, 0), axis=1),
        ]
    send_meta = jnp.stack(columns, axis=1)

    def own(table):
        return lax.dynamic_index_in_dim(table, me, 0, keepdims=False)

    own_source, own_low, own_high = own(source), own(low), own(high)
    own_lists, own_live = own(lists), own(live)
    earlier = (own_source[None, :] == own_source[:, None]) & (number < number.T)
    rank = jnp.minimum(jnp.any(earlier, axis=1).astype(jnp.int32), per_source - 1)
    recv_meta = jnp.stack([(me - own_source + blocks) % blocks, LIST * rank], axis=0)
    in_time, in_rows = window_time > 0, window_rows > 0
    rows = [in_time, in_rows, in_time & in_rows]
    for tile in range(ROW_TILES):
        for wanted in (own_low, own_high):
            found = own_live[tile] & (own_lists[tile] == wanted[:, None])
            rows.append(jnp.any(found, axis=1))
    biases = jnp.where(jnp.stack(rows, axis=0), 0.0, BIG_NEG).astype(jnp.float32)
    return send_meta, recv_meta, biases


def on_device(queries, keys, values, block_list, list_len, window_time, window_rows):
    tiles, tok, feat = queries.shape
    heads = window_time.shape[0]
    dim = feat // heads
    blocks = lax.axis_size("seq")
    per_source = (heads + blocks - 2) // (blocks - 1)
    chunks = heads // CHUNK_HEADS
    send_meta, recv_meta, biases = listed(
        block_list, list_len, window_time, window_rows, blocks, heads, per_source
    )
    kind = keys.dtype
    smem = pl.BlockSpec(memory_space=pltpu.SMEM)
    vmem = pl.BlockSpec(memory_space=pltpu.VMEM)
    anywhere = pl.BlockSpec(memory_space=pl.ANY)
    dma = pltpu.SemaphoreType.DMA
    return pl.pallas_call(
        functools.partial(kernel, blocks, heads, tok, dim, per_source),
        out_shape=jax.ShapeDtypeStruct(queries.shape, queries.dtype),
        in_specs=[smem, smem, smem, anywhere, anywhere, anywhere],
        out_specs=vmem,
        scratch_shapes=[
            pltpu.VMEM((heads, tiles, tok, dim), kind),
            pltpu.VMEM((2, heads, tiles, tok, dim), kind),
            pltpu.VMEM((2, heads, tok, dim), kind),
            pltpu.VMEM((2, heads, tiles, tok, dim), kind),
            pltpu.VMEM((2, heads, tok, dim), kind),
            pltpu.VMEM((2, heads, tiles, tok, dim), kind),
            pltpu.VMEM((2, heads, tok, dim), kind),
            pltpu.VMEM((blocks, per_source * LIST, 2, tok, dim), kind),
            pltpu.VMEM((blocks, per_source * LIST, 2, tok, dim), kind),
            pltpu.VMEM((heads, tiles, tok, dim), jnp.float32),
            pltpu.VMEM((heads, tiles, tok, 1), jnp.float32),
            pltpu.VMEM((heads, tiles, tok, 1), jnp.float32),
            dma((3, heads)),
            dma((2,)),
            dma((chunks, 2)),
            dma((chunks, 2)),
            dma((chunks, 2)),
            dma((chunks, 2)),
            dma((blocks, 2)),
        ],
        compiler_params=pltpu.CompilerParams(
            collective_id=0, has_side_effects=True, vmem_limit_bytes=56 * 1024 * 1024
        ),
        cost_estimate=pl.CostEstimate(
            flops=4 * heads * tiles * 10 * tok * tok * dim,
            bytes_accessed=4 * tiles * tok * feat * 2,
            transcendentals=heads * tiles * 10 * tok * tok,
        ),
    )(send_meta, recv_meta, biases, queries, keys, values)


def solution(mesh):
    return jax.shard_map(
        on_device,
        mesh=mesh,
        in_specs=(
            P(("group", "seq"), None, None),
            P(("group", "seq"), None, None),
            P(("group", "seq"), None, None),
            P("group", None, None),
            P("group", None),
            P(),
            P(),
        ),
        out_specs=P(("group", "seq"), None, None),
        check_vma=False,
    )
```

time: 678 us -> 217 us (0.32); the launches traced: 666 us -> 217 us
  local copies, waits for them, and re-layouts: 214 us -> 6.03 us
  Pallas kernels: 0 us -> 207 us
  other arithmetic: 159 us -> 3.36 us
  waiting for transfers between devices: 137 us -> 0 us
  matrix products: 118 us -> 0 us
  starting transfers between devices: 24.3 us -> 0 us
  loops' own time: 14 us -> 0 us
    pallas_call x0 -> x1, Pallas kernels: none -> 207 us  [on_device(): pl.pallas_call(functools.partial(kernel, blocks, heads, tok, dim, per_sou...]
    ppermute x6 -> x0, waiting for transfers between devices: 137 us -> none  [the longest x4 137 us: passed_along(): lax.ppermute(value, axis, [(source, source + steps) for source in range(i...]
    concatenate x7 -> x0, other arithmetic: 121 us -> none  [the longest x1 60.3 us: on_device(): jnp.concatenate([key_heads[:, a:a + TIME_TILES] for a in range(3)], axis=2)]
    dot_general x80 -> x0, matrix products: 118 us -> none  [the longest x20 36.9 us: one_head(): jnp.einsum('tqd,tkd->tqk', query_one, key_win, preferred_element_type=jnp...]
    reshape x7 -> x0, local copies, waits for them, and re-layouts: 49.6 us -> none  [the longest x2 34.3 us: head_major(): extended.reshape(TIME_TILES + 2, ext_cols * tile_len, heads, head_dim)]
    dynamic_slice x65 -> x1, local copies, waits for them, and re-layouts: 47.2 us -> 0.01 us  [own(): return lax.dynamic_index_in_dim(table, me, 0, keepdims=False)]
    dynamic_update_slice x44 -> x0, local copies, waits for them, and re-layouts: 29.5 us -> none  [the longest x40 15.7 us: on_device(): lax.map(one_head, (query_heads, key_windows, val_windows, far_key_heads,...]
    unnamed x19 -> x3, local copies, waits for them, and re-layouts: 30 us -> 4.55 us
  transfers between devices with their start and end apart: 8 -> 0, of which waited for: 1 -> 0; matrix products, arithmetic and copies ran while one was open for 39% -> 0% of each run, Pallas kernels for 0% -> 0%
where the time goes in v1:
time: 217 us
  Pallas kernels  207 us (95%)
  local copies, waits for them, and re-layouts  6.03 us (3%)
  other arithmetic  3.36 us (2%)
    pallas_call x1, Pallas kernels, on_device(): pl.pallas_call(functools.partial(kernel, blocks, heads, tok, dim, per_sou...  207 us
    unnamed x3, local copies, waits for them, and re-layouts  4.55 us

profile of v1, /device:TPU:13, one launch (start us, length us, event | category | flops | bytes accessed | tf_op | source)
XLA Modules:
  0.0 216.9 jit_solution(11188777233028160718)
XLA Ops:
  0.0 0.7 and_bitcast_fusion
  0.7 0.8 copy.46
  1.5 0.8 select_reduce_fusion
  2.3 0.1 copy.40
  2.5 0.1 copy.37
  2.7 0.1 select_reduce_fusion.4
  2.8 0.2 select_reduce_fusion.3
  3.0 0.2 fusion.1
  3.2 0.6 pad_add_fusion.recv_meta
  3.8 0.1 copy.41
  3.9 0.1 copy.44
  4.0 0.1 copy.42
  4.1 0.1 copy.45
  4.2 0.1 copy.38
  4.2 0.1 copy.43
  4.3 0.7 stack.54.send_meta
  5.0 0.8 copy.47
  5.9 0.1 stack.65
  5.9 0.6 broadcast_select_fusion.biases
  6.5 207.4 %shard_map.73 = bf16[3,128,2560]{2,1,0:T(8,128)(2,1)} custom-call(s32[16,6]{1,0:T(8,128)} %stack.54.send_meta, s32[2,20]{1,0:T(2,128)} %pad_add_fusion.recv_meta, f32[9,20]{1,0:T(8,128)} %broadcast_select_fusion.biases, bf16[3,128,2560]{2,1,0:T(8,128)(2,1)} %q_hbm.1, bf16[3,128,2560]{2,1,0:T(8,128)(2,1)} %k_hbm.1, bf16[3,128,2560]{2,1,0:T(8,128)(2,1)} %v_hbm.1), custom_call_target="tpu_custom_call" | custom-call | flops 5033164800 | bytes 7864320 | tf_op jit(solution)/shard_map/pallas_call | solution.py:338
  213.9 2.9 %copy.49 = bf16[3,128,2560]{2,1,0:T(8,128)(2,1)} copy(bf16[3,128,2560]{2,1,0:T(8,128)(2,1)} %shard_map.73) | data formatting | bytes 3932160
  (14 shorter events, 0.2 us)

commit v2 on v1

--- a/solution.py
+++ b/solution.py
@@ -11,15 +11,15 @@
 ROW_TILES = 3
 ROW_BLOCKS = 2
 LIST = 2
-CHUNK_HEADS = 4
+REACH_STEPS = (8, 10, 12, 14)
 BIG_NEG = -1e30
 
 
 def kernel(
-    blocks, heads, tok, dim, per_source,
-    send_meta, recv_meta, biases, q_hbm, k_hbm, v_hbm, out_ref,
-    qs, kv, edge, near, near_edge, relayed, relayed_edge, far_out, far_in, acc, top, total,
-    load_sem, edge_sem, near_sem, near_edge_sem, relay_sem, relay_edge_sem, far_sem,
+    blocks, heads, tok, dim, per_source, chunk_heads, chunks, detours,
+    send_meta, recv_meta, order, biases, q_hbm, k_hbm, v_hbm, out_ref,
+    qs, kv, packed, edge, passing, near, near_edge, relayed, relayed_edge, far_out, far_in, acc, top, total,
+    load_sem, edge_sem, pass_sem, near_sem, near_edge_sem, relay_sem, relay_edge_sem, far_sem,
 ):
     me = lax.axis_index("seq")
     side = lax.rem(me, ROW_BLOCKS)
@@ -34,7 +34,7 @@
     relay_to = me + ROW_BLOCKS * ahead
     edge_tile = 2 - 2 * side
     other_tile = 2 * side
-    chunks = heads // CHUNK_HEADS
+    direct = chunks - detours
 
     def remote(src, dst, sems, device):
         return pltpu.make_async_remote_copy(
@@ -43,17 +43,29 @@
         )
 
     def part_of(chunk):
-        return pl.ds(chunk * CHUNK_HEADS, CHUNK_HEADS)
+        return pl.ds(chunk * chunk_heads, chunk_heads)
 
     def near_copy(chunk):
         part = part_of(chunk)
-        return remote(kv.at[:, part], near.at[:, part], near_sem.at[chunk], mirror)
+        return remote(packed.at[:, part], near.at[:, part], near_sem.at[chunk], mirror)
 
     def near_edge_copy(chunk):
         part = part_of(chunk)
         return remote(
             near.at[:, part, edge_tile], near_edge.at[:, part],
             near_edge_sem.at[chunk], partner,
+        )
+
+    def pass_copy(chunk):
+        return remote(
+            packed.at[:, part_of(direct + chunk)], passing.at[:, part_of(chunk)],
+            pass_sem.at[chunk], me - ROW_BLOCKS * ahead,
+        )
+
+    def pass_on_copy(chunk):
+        return remote(
+            passing.at[:, part_of(chunk)], relayed.at[:, part_of(direct + chunk)],
+            relay_sem.at[direct + chunk], mirror,
         )
 
     def relay_copy(chunk):
@@ -113,6 +125,20 @@
     def start_near(chunk, carry):
         near_copy(chunk).start()
         return carry
+
+    def pack(index, carry):
+        head = order[0, index]
+        for part in range(2):
+            for tile in range(ROW_TILES):
+                packed[part, index, tile] = kv[part, head, tile]
+        return carry
+
+    lax.fori_loop(0, chunks * chunk_heads, pack, 0)
+
+    @pl.when(takes)
+    def _():
+        for chunk in range(detours):
+            pass_copy(chunk).start()
 
     lax.fori_loop(0, chunks, start_near, 0)
 
@@ -156,14 +182,16 @@
     def keep(head, tile, state):
         top[head, tile], total[head, tile], acc[head, tile] = state
 
-    def window_row(head, rows, edges, own):
+    def window_row(index, rows, edges, own):
+        head = order[0, index]
+        spot = head if own else index
         along = jnp.float32(0.0) if own else biases[0, head]
         lane = lax.broadcasted_iota(jnp.int32, (1, 3 * tok), 1)
         bias = jnp.where(lane < tok, along, biases[1 if own else 2, head])
-        k_mid, v_mid = rows[0, head, 1], rows[1, head, 1]
-        k_edge, v_edge = rows[0, head, edge_tile], rows[1, head, edge_tile]
-        k_other, v_other = rows[0, head, other_tile], rows[1, head, other_tile]
-        k_out, v_out = edges[0, head], edges[1, head]
+        k_mid, v_mid = rows[0, spot, 1], rows[1, spot, 1]
+        k_edge, v_edge = rows[0, spot, edge_tile], rows[1, spot, edge_tile]
+        k_other, v_other = rows[0, spot, other_tile], rows[1, spot, other_tile]
+        k_out, v_out = edges[0, spot], edges[1, spot]
         for tile, key, value in (
             (1, (k_mid, k_edge, k_other), (v_mid, v_edge, v_other)),
             (edge_tile, (k_edge, k_mid, k_out), (v_edge, v_mid, v_out)),
@@ -172,7 +200,7 @@
             key = jnp.concatenate(key, axis=0)
             value = jnp.concatenate(value, axis=0)
             scores = scores_of(qs[head, tile], key, bias[:, : key.shape[0]])
-            keep(head, tile, fold(head, tile, scores, value, own))
+            keep(index, tile, fold(index, tile, scores, value, own))
 
     edge_copy.wait_recv()
 
@@ -184,17 +212,17 @@
 
     def near_rows(chunk):
         def step(inner, carry):
-            window_row(chunk * CHUNK_HEADS + inner, near, near_edge, False)
+            window_row(chunk * chunk_heads + inner, near, near_edge, False)
             return carry
 
-        lax.fori_loop(0, CHUNK_HEADS, step, 0)
+        lax.fori_loop(0, chunk_heads, step, 0)
 
     def relayed_rows(chunk):
         def step(inner, carry):
-            window_row(chunk * CHUNK_HEADS + inner, relayed, relayed_edge, False)
+            window_row(chunk * chunk_heads + inner, relayed, relayed_edge, False)
             return carry
 
-        lax.fori_loop(0, CHUNK_HEADS, step, 0)
+        lax.fori_loop(0, chunk_heads, step, 0)
 
     def relay_arrived(chunk):
         relay_copy(chunk).wait_recv()
@@ -208,9 +236,14 @@
         near_copy(chunk).wait_recv()
         near_edge_copy(chunk).start()
 
-        @pl.when(gives)
+        @pl.when(jnp.logical_and(gives, chunk < direct))
         def _():
             relay_copy(chunk).start()
+
+        @pl.when(jnp.logical_and(gives, jnp.logical_and(chunk > 0, chunk <= detours)))
+        def _():
+            pass_copy(chunk - 1).wait_recv()
+            pass_on_copy(chunk - 1).start()
 
         @pl.when(jnp.logical_and(takes, chunk > 0))
         def _():
@@ -247,7 +280,7 @@
         for tile in range(ROW_TILES):
             bias = jnp.where(lane < tok, biases[3 + 2 * tile, head], biases[4 + 2 * tile, head])
             scores = scores_of(qs[head, tile], key, bias)
-            _, amount, mixed = fold(head, tile, scores, value, False)
+            _, amount, mixed = fold(order[1, head], tile, scores, value, False)
             out_ref[tile, :, cols] = (mixed / amount).astype(out_ref.dtype)
         return carry
 
@@ -259,9 +292,17 @@
         near_copy(chunk).wait_send()
         near_edge_copy(chunk).wait_send()
 
-        @pl.when(gives)
+        @pl.when(jnp.logical_and(gives, chunk < direct))
         def _():
             relay_copy(chunk).wait_send()
+
+        @pl.when(jnp.logical_and(gives, chunk < detours))
+        def _():
+            pass_on_copy(chunk).wait_send()
+
+        @pl.when(jnp.logical_and(takes, chunk < detours))
+        def _():
+            pass_copy(chunk).wait_send()
 
         @pl.when(takes)
         def _():
@@ -317,7 +358,14 @@
             found = own_live[tile] & (own_lists[tile] == wanted[:, None])
             rows.append(jnp.any(found, axis=1))
     biases = jnp.where(jnp.stack(rows, axis=0), 0.0, BIG_NEG).astype(jnp.float32)
-    return send_meta, recv_meta, biases
+    rank = jnp.sum(
+        (window_time[None, :] > window_time[:, None])
+        | ((window_time[None, :] == window_time[:, None]) & (number < number.T)),
+        axis=1,
+        dtype=jnp.int32,
+    )
+    head_at = jnp.sum(jnp.where(rank[None, :] == number.T, number, 0), axis=1)
+    return send_meta, recv_meta, jnp.stack([head_at, rank], axis=0), biases
 
 
 def on_device(queries, keys, values, block_list, list_len, window_time, window_rows):
@@ -326,28 +374,48 @@
     dim = feat // heads
     blocks = lax.axis_size("seq")
     per_source = (heads + blocks - 2) // (blocks - 1)
-    chunks = heads // CHUNK_HEADS
-    send_meta, recv_meta, biases = listed(
+    meta = listed(
         block_list, list_len, window_time, window_rows, blocks, heads, per_source
     )
+    steps = [count for count in REACH_STEPS if count < heads] + [heads]
+    reaching = jnp.sum((window_time > 0).astype(jnp.int32))
+    branch = sum((reaching > count).astype(jnp.int32) for count in steps[:-1])
+    calls = [
+        functools.partial(attend, count, number, blocks, heads, per_source)
+        for number, count in enumerate(steps)
+    ]
+    return lax.switch(branch, calls, *meta, queries, keys, values)
+
+
+def attend(reaching, number, blocks, heads, per_source, *operands):
+    queries, keys = operands[-3:-1]
+    tiles, tok, feat = queries.shape
+    dim = feat // heads
+    chunk_heads = 4 if reaching == 20 else 2
+    chunks = reaching // chunk_heads
+    detours = 2 * chunks // 5
     kind = keys.dtype
     smem = pl.BlockSpec(memory_space=pltpu.SMEM)
     vmem = pl.BlockSpec(memory_space=pltpu.VMEM)
     anywhere = pl.BlockSpec(memory_space=pl.ANY)
     dma = pltpu.SemaphoreType.DMA
     return pl.pallas_call(
-        functools.partial(kernel, blocks, heads, tok, dim, per_source),
+        functools.partial(
+            kernel, blocks, heads, tok, dim, per_source, chunk_heads, chunks, detours
+        ),
         out_shape=jax.ShapeDtypeStruct(queries.shape, queries.dtype),
-        in_specs=[smem, smem, smem, anywhere, anywhere, anywhere],
+        in_specs=[smem] * 4 + [anywhere] * 3,
         out_specs=vmem,
         scratch_shapes=[
             pltpu.VMEM((heads, tiles, tok, dim), kind),
             pltpu.VMEM((2, heads, tiles, tok, dim), kind),
+            pltpu.VMEM((2, reaching, tiles, tok, dim), kind),
             pltpu.VMEM((2, heads, tok, dim), kind),
-            pltpu.VMEM((2, heads, tiles, tok, dim), kind),
-            pltpu.VMEM((2, heads, tok, dim), kind),
-            pltpu.VMEM((2, heads, tiles, tok, dim), kind),
-            pltpu.VMEM((2, heads, tok, dim), kind),
+            pltpu.VMEM((2, detours * chunk_heads, tiles, tok, dim), kind),
+            pltpu.VMEM((2, reaching, tiles, tok, dim), kind),
+            pltpu.VMEM((2, reaching, tok, dim), kind),
+            pltpu.VMEM((2, reaching, tiles, tok, dim), kind),
+            pltpu.VMEM((2, reaching, tok, dim), kind),
             pltpu.VMEM((blocks, per_source * LIST, 2, tok, dim), kind),
             pltpu.VMEM((blocks, per_source * LIST, 2, tok, dim), kind),
             pltpu.VMEM((heads, tiles, tok, dim), jnp.float32),
@@ -355,6 +423,7 @@
             pltpu.VMEM((heads, tiles, tok, 1), jnp.float32),
             dma((3, heads)),
             dma((2,)),
+            dma((detours, 2)),
             dma((chunks, 2)),
             dma((chunks, 2)),
             dma((chunks, 2)),
@@ -362,14 +431,14 @@
             dma((blocks, 2)),
         ],
         compiler_params=pltpu.CompilerParams(
-            collective_id=0, has_side_effects=True, vmem_limit_bytes=56 * 1024 * 1024
+            collective_id=number, has_side_effects=True, vmem_limit_bytes=56 * 1024 * 1024
         ),
         cost_estimate=pl.CostEstimate(
             flops=4 * heads * tiles * 10 * tok * tok * dim,
             bytes_accessed=4 * tiles * tok * feat * 2,
             transcendentals=heads * tiles * 10 * tok * tok,
         ),
-    )(send_meta, recv_meta, biases, queries, keys, values)
+    )(*operands)
 
 
 def solution(mesh):

time: 217 us -> 167 us (0.77)
  Pallas kernels: 207 us -> 154 us
  between operations: 0.08 us -> 2.68 us
    pallas_call x1, Pallas kernels: 207 us -> 154 us  [attend(): pl.pallas_call(functools.partial(kernel, blocks, heads, tok, dim, per_sou...]
    reduce_sum x0 -> x3, other arithmetic: none -> 2.32 us  [the longest x1 1.29 us: on_device(): reaching = jnp.sum((window_time > 0).astype(jnp.int32))]
where the time goes in v2:
time: 167 us; the launch traced here: 166 us
  Pallas kernels  154 us (92%)
  other arithmetic  5.11 us (3%)
  local copies, waits for them, and re-layouts  3.9 us (2%)
  between operations  2.68 us (2%)
    pallas_call x1, Pallas kernels, attend(): pl.pallas_call(functools.partial(kernel, blocks, heads, tok, dim, per_sou...  154 us

profile of v2, /device:TPU:13, one launch (start us, length us, event | category | flops | bytes accessed | tf_op | source)
XLA Modules:
  0.0 166.3 jit_solution(5141921934023526281)
XLA Ops:
  0.0 1.3 convert_reduce_fusion.1
  3.9 0.9 convert_reduce_fusion
  4.8 0.1 select_reduce_fusion.2
  4.9 0.7 and_bitcast_fusion
  5.6 0.8 copy.73
  6.4 0.8 select_reduce_fusion
  7.3 0.1 copy.72
  7.4 0.1 copy.71
  7.6 0.1 select_reduce_fusion.5
  7.7 0.2 select_reduce_fusion.4
  8.0 0.2 fusion.2
  8.2 0.8 copy.74
  9.1 0.1 stack.74
  9.1 155.9 %conditional.1 = (bf16[3,128,2560]{2,1,0:T(8,128)(2,1)S(1)}) conditional(s32[]{:T(128)} %clamp.3, (s32[16,6]{0,1:T(8,128)S(1)}, s32[2,20]{1,0:T(2,128)S(1)}, s32[2,20]{1,0:T(2,128)S(1)}, pred[9,20]{1,0:T(8,128)(4,1)S(1)}, bf16[3,128,2560]{2,1,0:T(8,128)(2,1)}, /*index=5*/bf16[3,128,2560]{2,1,0:T(8,128)(2,1)}, ...), branch_computations={%region_20.21_spmd.clone, %region_21.22_spmd.clone, %region_22.23_... | conditional | flops 5033164800 | bytes 7865996 | solution.py:387
  9.1 0.6 broadcast_select_fusion.1.biases
  9.7 0.7 copy.76.send_meta
  10.4 154.4 %branch_1_fun.1 = bf16[3,128,2560]{2,1,0:T(8,128)(2,1)S(1)} custom-call(s32[16,6]{1,0:T(8,128)} %copy.76.send_meta, s32[2,20]{1,0:T(2,128)S(1)} %get-tuple-element.187.recv_meta, s32[2,20]{1,0:T(2,128)S(1)} %get-tuple-element.188.order, f32[9,20]{1,0:T(8,128)} %broadcast_select_fusion.1.biases, bf16[3,128,2560]{2,1,0:T(8,128)(2,1)} %get-tuple-element.190.q_hbm, ...), custom_call_target="tpu_custom_call" | custom-call | flops 5033164800 | bytes 7864320 | tf_op jit(solution)/shard_map/cond/branch_1_fun/pallas_call | solution.py:402
  165.0 1.3 copy.86
  (16 shorter events, 0.3 us)
